TPU v7x, 32 devices: a whole 2x2x4 slice. The times are simulated.
32 devices in a mesh: sub: 8 (over z, y), mode: 4 (over x, core).
Axes of the slice: x: 2, y: 2, z: 4, core: 2. Of those that a mesh axis runs over, the one named last changes fastest.
Arguments:
- panels: bfloat16 [8, 2048, 768], P('sub', 'mode'), may hold values from -0.59765625 to 0.59765625
- eigvals: float32 [8, 2048], P('sub', 'mode'), may hold values from 0.5 to 20
- counts: int32 [8], P('sub'), may hold values from 512 to 2048, as said below
- separator_diag: float32 [8, 768], P('sub'), may hold values from 4 to 8
- separator_index_tables: int32 [8, 768], replicated, may hold values from 0 to 767, each once within a row
Outputs:
- condensed: float32 [768, 768], P('sub')
Inputs may be any that keep to these rules, and one draw needn't show every extreme that they name: `counts`: every value from 512 to 2048 can occur, and both ends occur in every draw. `separator_index_tables`: each row is a permutation of 0 to 767.
All inputs are finite; a program needn't handle non-finite values.
Results may differ from a plain program's by a relative error of at most 0.0003.
Values sent between devices are 32-bit elements; how exact they have to be, the bound alone decides.
A program may use at most 64 MiB of HBM per device.

v0:
```python
import math
import jax
import jax.numpy as jnp
from jax import lax
from jax.sharding import PartitionSpec as P


def from_partner(array, axis, stride):
    return lax.ppermute(array, axis, [(i, i ^ 1 << stride) for i in range(lax.axis_size(axis))])


def select_permutation(separator_index_tables, level_number, tree_node_index):
    span_rows = 2**level_number
    map_row = tree_node_index * span_rows + span_rows - 1
    base_perm = lax.dynamic_index_in_dim(separator_index_tables, map_row, 0, keepdims=False)
    sep_width = separator_index_tables.shape[1]
    shifted = (jnp.arange(sep_width, dtype=jnp.int32) + 97 * level_number % sep_width) % sep_width
    return jnp.take(base_perm, shifted)


def relabel_equations(schur_remainder_patch, arrangement_list):
    rows_first = jnp.take(schur_remainder_patch, arrangement_list, axis=0)
    return jnp.take(rows_first.T, arrangement_list, axis=0).T


def local(panels, eigvals, counts, separator_diag, separator_index_tables):
    sub_here = lax.axis_index("sub")
    mode_here = lax.axis_index("mode")
    sub_dev = panels.shape[0]
    mode_dev = panels.shape[1]
    sep_width = panels.shape[2]
    mode_start = mode_here * mode_dev
    diag_on = (mode_here == 0).astype(jnp.float32)
    contract = (((0,), (0,)), ((), ()))
    first_leaf = sub_here * sub_dev
    stack_nodes = []
    panel_rows = panels[0]
    live_count = counts[0]
    live_mask = (mode_start + jnp.arange(mode_dev, dtype=jnp.int32) < live_count).astype(
        jnp.float32
    )
    weighted = (panel_rows.astype(jnp.float32) * (live_mask / eigvals[0])[:, None]).astype(
        jnp.bfloat16
    )
    partial_sum = lax.dot_general(
        weighted, panel_rows, contract, preferred_element_type=jnp.float32
    )
    stack_nodes.append((0, diag_on * jnp.diag(separator_diag[0]) - partial_sum))
    while len(stack_nodes) >= 2 and stack_nodes[-1][0] == stack_nodes[-2][0]:
        level_number, right_matrix_tile = stack_nodes.pop()
        level_same, left_matrix_tile = stack_nodes.pop()
        span_leaves = 2 ** (level_number + 1)
        left_child_node = first_leaf // 2**level_number + 2 * ((1 - span_leaves) // span_leaves)
        reordered_first_factor = relabel_equations(
            left_matrix_tile,
            select_permutation(separator_index_tables, level_number, left_child_node),
        )
        reordered_second_factor = relabel_equations(
            right_matrix_tile,
            select_permutation(separator_index_tables, level_number, left_child_node + 1),
        )
        stack_nodes.append((level_number + 1, reordered_first_factor + reordered_second_factor))
    device_level_count, schur_remainder_patch = stack_nodes[0]
    sub_count = lax.axis_size("sub")
    sub_bits = sub_count.bit_length() - 1
    schur_remainder_patch = lax.psum(schur_remainder_patch, "mode")
    for bit_position in range(sub_bits):
        tree_node_index = sub_here // 2**bit_position
        schur_remainder_patch = relabel_equations(
            schur_remainder_patch,
            select_permutation(
                separator_index_tables, device_level_count + bit_position, tree_node_index
            ),
        )
        schur_remainder_patch = schur_remainder_patch + from_partner(
            schur_remainder_patch, "sub", bit_position
        )
    own_rows = sep_width // sub_count
    own_block = lax.dynamic_slice_in_dim(schur_remainder_patch, sub_here * own_rows, own_rows, 0)
    return own_block * (1.0 / math.sqrt(sub_dev * sub_count))


def solution(mesh):
    return jax.shard_map(
        local,
        mesh=mesh,
        in_specs=(P("sub", "mode", None), P("sub", "mode"), P("sub"), P("sub", None), P()),
        out_specs=P("sub", None),
        check_vma=False,
    )
```

profile of v0, /device:TPU:0, one launch (start us, length us, event | category | flops | bytes accessed | tf_op | source)
XLA Modules:
  0.0 345.9 jit_solution(12305404054721332280)
XLA Ops:
  8.6 3.7 %multiply_subtract_fusion = f32[768,768]{1,0:T(8,128)} fusion(f32[768]{0:T(1024)S(1)} %reduce.3, f32[]{:T(128)S(6)} %convert_element_type.20, bf16[1,512,768]{2,1,0:T(8,128)(2,1)} %param.9, f32[512]{0:T(512)S(1)} %convert_divide_fusion), kind=kOutput, calls=%fused_computation.15 | convolution fusion | flops 607518720 | bytes 3150852 | tf_op jit(solution)/shard_map/dot_general | solution.py:45
  13.3 3.2 gather_fusion
  16.5 54.3 %all-reduce.2.cloned.1.call-done = f32[768,768]{1,0:T(8,128)} async-done(((f32[768,768]{1,0:T(8,128)}), f32[768,768]{1,0:T(8,128)}) %all-reduce.2.cloned.1.call-update) | async-done | bytes 2359312 | tf_op jit(solution)/shard_map/psum | solution.py:66
  70.8 5.1 %gather_fusion.1 = f32[768,768]{1,0:T(8,128)S(1)} fusion(f32[768,768]{1,0:T(8,128)} %all-reduce.2.cloned.1.call-done, s32[1024]{0:T(1024)S(1)} %pad_clamp_fusion.2), kind=kCustom, calls=%fused_computation.1.clone | custom fusion | bytes 4721664 | tf_op jit(solution)/shard_map/jit(_take)/gather | solution.py:22
  77.6 2.0 copy.18
  79.7 3.5 %gather_fusion.2 = f32[768,768]{1,0:T(8,128)} fusion(f32[768,768]{1,0:T(8,128)S(1)} %copy.18, s32[1024]{0:T(1024)S(1)} %pad_clamp_fusion.2), kind=kCustom, calls=%fused_computation.4.clone | custom fusion | bytes 4721664 | tf_op jit(solution)/shard_map/jit(_take)/gather | solution.py:23
  83.1 3.3 select_bitcast_fusion.4
  88.0 3.2 gather_fusion.3
  91.2 48.5 %collective-permute-done = f32[768,768]{0,1:T(8,128)} collective-permute-done((f32[768,768]{0,1:T(8,128)}, f32[768,768]{0,1:T(8,128)}, u32[]{:S(2)}, u32[]{:S(2)}) %collective-permute-start) | collective-permute-done | bytes 2359328 | tf_op jit(solution)/shard_map/ppermute | solution.py:9
  139.7 3.5 %fusion.12 = f32[768,768]{0,1:T(8,128)} fusion(f32[768,768]{0,1:T(8,128)} %collective-permute-done, f32[768,768]{1,0:T(8,128)S(1)} %copy-done.1, pred[768]{0:T(1024)(128)(4,1)S(1)} %compare_and_fusion.2), kind=kLoop, calls=%fused_computation.53 | loop fusion | flops 1179648 | bytes 7078656 | tf_op jit(solution)/shard_map/add | solution.py:75
  143.2 2.0 copy.19
  145.2 3.5 %gather_fusion.4 = f32[768,768]{1,0:T(8,128)} fusion(f32[768,768]{1,0:T(8,128)S(1)} %copy.19, s32[1024]{0:T(1024)S(1)} %pad_clamp_fusion.1), kind=kCustom, calls=%fused_computation.5.clone | custom fusion | bytes 4721664 | tf_op jit(solution)/shard_map/jit(_take)/gather | solution.py:22
  148.7 3.3 select_bitcast_fusion.3
  152.0 2.0 copy.20
  154.0 3.5 %gather_fusion.5 = f32[768,768]{1,0:T(8,128)} fusion(f32[768,768]{1,0:T(8,128)S(1)} %copy.20, s32[1024]{0:T(1024)S(1)} %pad_clamp_fusion.1), kind=kCustom, calls=%fused_computation.6.clone | custom fusion | bytes 4721664 | tf_op jit(solution)/shard_map/jit(_take)/gather | solution.py:23
  157.5 3.3 select_bitcast_fusion.2
  162.3 3.2 gather_fusion.6
  165.6 47.6 %collective-permute-done.1 = f32[768,768]{0,1:T(8,128)} collective-permute-done((f32[768,768]{0,1:T(8,128)}, f32[768,768]{0,1:T(8,128)}, u32[]{:S(2)}, u32[]{:S(2)}) %collective-permute-start.1) | collective-permute-done | bytes 2359328 | tf_op jit(solution)/shard_map/ppermute | solution.py:9
  213.2 3.4 fusion.11
  218.6 3.5 %gather_fusion.7 = f32[768,768]{1,0:T(8,128)} fusion(f32[768,768]{1,0:T(8,128)S(1)} %copy.21, s32[1024]{0:T(1024)S(1)} %pad_clamp_fusion), kind=kCustom, calls=%fused_computation.7.clone | custom fusion | bytes 4721664 | tf_op jit(solution)/shard_map/jit(_take)/gather | solution.py:22
  222.1 3.3 select_bitcast_fusion.1
  227.5 3.5 %gather_fusion.8 = f32[768,768]{1,0:T(8,128)} fusion(f32[768,768]{1,0:T(8,128)S(1)} %copy.22, s32[1024]{0:T(1024)S(1)} %pad_clamp_fusion), kind=kCustom, calls=%fused_computation.8.clone | custom fusion | bytes 4721664 | tf_op jit(solution)/shard_map/jit(_take)/gather | solution.py:23
  234.5 2.4 collective-permute-start.2
  236.9 100.4 %collective-permute-done.2 = f32[768,768]{1,0:T(8,128)S(1)} collective-permute-done((f32[768,768]{1,0:T(8,128)}, f32[768,768]{1,0:T(8,128)S(1)}, u32[]{:S(2)}, u32[]{:S(2)}) %collective-permute-start.2) | collective-permute-done | bytes 2359328 | tf_op jit(solution)/shard_map/ppermute | solution.py:9
  (32 shorter events, 16.4 us)
Async XLA Ops:
  6.5 64.3 %all-reduce.2.cloned.1.call-start = ((), (), s32[]{:S(2)}) async-start(), calls=%async_computation | async-start | bytes 4718592 | tf_op jit(solution)/shard_map/psum | solution.py:66
  86.5 53.2 %copy-start.1 = (f32[768,768]{1,0:T(8,128)S(1)}, f32[768,768]{1,0:T(8,128)}, u32[]{:S(2)}) copy-start(f32[768,768]{1,0:T(8,128)} %gather_fusion.2) | copy-start | bytes 7077892
  86.5 53.2 %collective-permute-start = (f32[768,768]{0,1:T(8,128)}, f32[768,768]{0,1:T(8,128)}, u32[]{:S(2)}, u32[]{:S(2)}) collective-permute-start(f32[768,768]{0,1:T(8,128)} %select_bitcast_fusion.4), channel_id=1, source_target_pairs={{0,4},{4,0},{8,12},{12,8},{16,20},{20,16},{24,28},{28,24},{1,5},{5... | collective-permute-start | bytes 7077896 | tf_op jit(solution)/shard_map/ppermute | solution.py:9
  160.8 52.3 %copy-start = (f32[768,768]{1,0:T(8,128)S(1)}, f32[768,768]{1,0:T(8,128)}, u32[]{:S(2)}) copy-start(f32[768,768]{1,0:T(8,128)} %gather_fusion.5) | copy-start | bytes 7077892
  160.8 52.3 %collective-permute-start.1 = (f32[768,768]{0,1:T(8,128)}, f32[768,768]{0,1:T(8,128)}, u32[]{:S(2)}, u32[]{:S(2)}) collective-permute-start(f32[768,768]{0,1:T(8,128)} %select_bitcast_fusion.2), channel_id=1, source_target_pairs={{0,8},{4,12},{8,0},{12,4},{16,24},{20,28},{24,16},{28,20},{1,9},{5... | collective-permute-start | bytes 7077896 | tf_op jit(solution)/shard_map/ppermute | solution.py:9
  234.5 102.8 %collective-permute-start.2 = (f32[768,768]{1,0:T(8,128)}, f32[768,768]{1,0:T(8,128)S(1)}, u32[]{:S(2)}, u32[]{:S(2)}) collective-permute-start(f32[768,768]{1,0:T(8,128)} %select_bitcast_fusion), channel_id=1, source_target_pairs={{0,16},{4,20},{8,24},{12,28},{16,0},{20,4},{24,8},{28,12},{1,17},{... | collective-permute-start | bytes 7077896 | tf_op jit(solution)/shard_map/ppermute | solution.py:9
Sparse Core Ops, SparseCore 0:
  12.5 58.3 all-reduce.1
where the time goes:
time: 347 us; the launch traced here: 346 us
  waiting for transfers between devices  251 us (72%)
  local copies, waits for them, and re-layouts  45.1 us (13%)
  other arithmetic  26.7 us (8%)
  between operations  14.2 us (4%)
  starting transfers between devices  5.37 us (2%)
  matrix products  3.73 us (1%)
    ppermute x3, waiting for transfers between devices, from_partner(): lax.ppermute(array, axis, [(i, i ^ 1 << stride) for i in range(lax.axis_s...  196 us
    psum x1, waiting for transfers between devices, local(): schur_remainder_patch = lax.psum(schur_remainder_patch, 'mode')  54.3 us
    transpose x6, other arithmetic, relabel_equations(): return jnp.take(rows_first.T, arrangement_list, axis=0).T  16.5 us
    gather x4, local copies, waits for them, and re-layouts, relabel_equations(): return jnp.take(rows_first.T, arrangement_list, axis=0).T  12.4 us
    gather x3, local copies, waits for them, and re-layouts, relabel_equations(): rows_first = jnp.take(schur_remainder_patch, arrangement_list, axis=0)  12.1 us
    gather x3, local copies, waits for them, and re-layouts, select_permutation(): return jnp.take(base_perm, shifted)  9.56 us
  transfers between devices with their start and end apart: 4, of which 4 were waited for; matrix products, arithmetic and copies ran while one was open for 3% of the time, Pallas kernels for 0%

commit v1 on v0

--- a/solution.py
+++ b/solution.py
@@ -63,7 +63,7 @@
     device_level_count, schur_remainder_patch = stack_nodes[0]
     sub_count = lax.axis_size("sub")
     sub_bits = sub_count.bit_length() - 1
-    schur_remainder_patch = lax.psum(schur_remainder_patch, "mode")
+    schur_remainder_patch = jnp.sum(lax.all_gather(schur_remainder_patch, "mode"), axis=0)
     for bit_position in range(sub_bits):
         tree_node_index = sub_here // 2**bit_position
         schur_remainder_patch = relabel_equations(

time: 347 us -> 362 us (1.043)
  waiting for transfers between devices: 251 us -> 261 us
  other arithmetic: 26.7 us -> 33 us
    all_gather x0 -> x1, waiting for transfers between devices: none -> 62.9 us  [local(): lax.all_gather(schur_remainder_patch, 'mode')]
    psum x1 -> x0, waiting for transfers between devices: 54.3 us -> none  [local(): schur_remainder_patch = lax.psum(schur_remainder_patch, 'mode')]
    reduce_sum x0 -> x1, other arithmetic: none -> 4.7 us  [local(): jnp.sum(lax.all_gather(schur_remainder_patch, 'mode'), axis=0)]
where the time goes in v1:
time: 362 us; the launch traced here: 361 us
  waiting for transfers between devices  261 us (72%)
  local copies, waits for them, and re-layouts  43.4 us (12%)
  other arithmetic  33 us (9%)
  between operations  14.2 us (4%)
  starting transfers between devices  5.37 us (1%)
  matrix products  3.72 us (1%)
    ppermute x3, waiting for transfers between devices, from_partner(): lax.ppermute(array, axis, [(i, i ^ 1 << stride) for i in range(lax.axis_s...  198 us
    all_gather x1, waiting for transfers between devices, local(): lax.all_gather(schur_remainder_patch, 'mode')  62.9 us
    transpose x6, other arithmetic, relabel_equations(): return jnp.take(rows_first.T, arrangement_list, axis=0).T  18.2 us
    gather x4, local copies, waits for them, and re-layouts, relabel_equations(): return jnp.take(rows_first.T, arrangement_list, axis=0).T  12.4 us
    gather x3, local copies, waits for them, and re-layouts, relabel_equations(): rows_first = jnp.take(schur_remainder_patch, arrangement_list, axis=0)  10.4 us
    gather x3, local copies, waits for them, and re-layouts, select_permutation(): return jnp.take(base_perm, shifted)  9.56 us
  transfers between devices with their start and end apart: 4, of which 4 were waited for; matrix products, arithmetic and copies ran while one was open for 3% of the time, Pallas kernels for 0%

profile of v1, /device:TPU:0, one launch (start us, length us, event | category | flops | bytes accessed | tf_op | source)
XLA Modules:
  0.0 360.8 jit_solution(11531159904679365215)
XLA Ops:
  8.6 3.7 %multiply_subtract_fusion = f32[768,768]{1,0:T(8,128)} fusion(f32[768]{0:T(1024)S(1)} %reduce.3, f32[]{:T(128)S(6)} %convert_element_type.20, bf16[1,512,768]{2,1,0:T(8,128)(2,1)} %param.9, f32[512]{0:T(512)S(1)} %convert_divide_fusion), kind=kOutput, calls=%fused_computation.15 | convolution fusion | flops 607518720 | bytes 3150852 | tf_op jit(solution)/shard_map/dot_general | solution.py:45
  13.3 3.2 gather_fusion
  16.5 62.9 %all-gather.3.cloned.1.call-done = f32[3072,768]{1,0:T(8,128)} async-done(((f32[768,768]{1,0:T(8,128)}), f32[3072,768]{1,0:T(8,128)}) %all-gather.3.cloned.1.call-update) | async-done | bytes 9437200 | tf_op jit(solution)/shard_map/all_gather | solution.py:66
  79.4 4.7 %reduce_sum.9 = f32[768,768]{1,0:T(8,128)S(1)} reduce(f32[4,768,768]{2,1,0:T(8,128)} %bitcast.26, f32[]{:T(128)} %constant.99.clone.1), dimensions={0}, to_apply=%region_0.1 | reduce | flops 1769472 | bytes 11796484 | tf_op jit(solution)/shard_map/reduce_sum | solution.py:66
  84.1 3.5 gather_fusion.1
  87.6 3.3 select_bitcast_fusion.5
  90.9 2.0 copy.18
  92.9 3.5 gather_fusion.2
  96.4 3.3 select_bitcast_fusion.4
  101.2 3.2 gather_fusion.3
  104.5 49.0 %collective-permute-done = f32[768,768]{0,1:T(8,128)} collective-permute-done((f32[768,768]{0,1:T(8,128)}, f32[768,768]{0,1:T(8,128)}, u32[]{:S(2)}, u32[]{:S(2)}) %collective-permute-start) | collective-permute-done | bytes 2359328 | tf_op jit(solution)/shard_map/ppermute | solution.py:9
  153.5 3.5 fusion.12
  159.0 3.5 gather_fusion.4
  162.5 3.3 select_bitcast_fusion.3
  167.8 3.5 gather_fusion.5
  171.3 3.3 select_bitcast_fusion.2
  176.1 3.2 gather_fusion.6
  179.4 48.2 %collective-permute-done.1 = f32[768,768]{0,1:T(8,128)} collective-permute-done((f32[768,768]{0,1:T(8,128)}, f32[768,768]{0,1:T(8,128)}, u32[]{:S(2)}, u32[]{:S(2)}) %collective-permute-start.1) | collective-permute-done | bytes 2359328 | tf_op jit(solution)/shard_map/ppermute | solution.py:9
  227.5 3.4 fusion.11
  233.0 3.5 gather_fusion.7
  236.5 3.3 select_bitcast_fusion.1
  241.8 3.5 gather_fusion.8
  248.9 2.4 collective-permute-start.2
  251.3 100.9 %collective-permute-done.2 = f32[768,768]{1,0:T(8,128)S(1)} collective-permute-done((f32[768,768]{1,0:T(8,128)}, f32[768,768]{1,0:T(8,128)S(1)}, u32[]{:S(2)}, u32[]{:S(2)}) %collective-permute-start.2) | collective-permute-done | bytes 2359328 | tf_op jit(solution)/shard_map/ppermute | solution.py:9
  (33 shorter events, 18.9 us)
Async XLA Ops:
  6.5 72.9 %all-gather.3.cloned.1.call-start = ((), (), s32[]{:S(2)}) async-start(), calls=%async_computation | async-start | bytes 11796480 | tf_op jit(solution)/shard_map/all_gather | solution.py:66
  99.7 53.7 %copy-start.1 = (f32[768,768]{1,0:T(8,128)S(1)}, f32[768,768]{1,0:T(8,128)}, u32[]{:S(2)}) copy-start(f32[768,768]{1,0:T(8,128)} %gather_fusion.2) | copy-start | bytes 7077892
  99.7 53.7 %collective-permute-start = (f32[768,768]{0,1:T(8,128)}, f32[768,768]{0,1:T(8,128)}, u32[]{:S(2)}, u32[]{:S(2)}) collective-permute-start(f32[768,768]{0,1:T(8,128)} %select_bitcast_fusion.4), channel_id=1, source_target_pairs={{0,4},{4,0},{8,12},{12,8},{16,20},{20,16},{24,28},{28,24},{1,5},{5... | collective-permute-start | bytes 7077896 | tf_op jit(solution)/shard_map/ppermute | solution.py:9
  174.6 52.9 %copy-start = (f32[768,768]{1,0:T(8,128)S(1)}, f32[768,768]{1,0:T(8,128)}, u32[]{:S(2)}) copy-start(f32[768,768]{1,0:T(8,128)} %gather_fusion.5) | copy-start | bytes 7077892
  174.6 52.9 %collective-permute-start.1 = (f32[768,768]{0,1:T(8,128)}, f32[768,768]{0,1:T(8,128)}, u32[]{:S(2)}, u32[]{:S(2)}) collective-permute-start(f32[768,768]{0,1:T(8,128)} %select_bitcast_fusion.2), channel_id=1, source_target_pairs={{0,8},{4,12},{8,0},{12,4},{16,24},{20,28},{24,16},{28,20},{1,9},{5... | collective-permute-start | bytes 7077896 | tf_op jit(solution)/shard_map/ppermute | solution.py:9
  248.9 103.3 %collective-permute-start.2 = (f32[768,768]{1,0:T(8,128)}, f32[768,768]{1,0:T(8,128)S(1)}, u32[]{:S(2)}, u32[]{:S(2)}) collective-permute-start(f32[768,768]{1,0:T(8,128)} %select_bitcast_fusion), channel_id=1, source_target_pairs={{0,16},{4,20},{8,24},{12,28},{16,0},{20,4},{24,8},{28,12},{1,17},{... | collective-permute-start | bytes 7077896 | tf_op jit(solution)/shard_map/ppermute | solution.py:9
Sparse Core Ops, SparseCore 0:
  12.4 66.9 all-gather.2
